TPU v7x, 256 devices: a whole 4x4x8 slice. The times are simulated.
256 devices in a mesh: opg: 16 (over z, x_lo), sec: 16 (over x_hi, y, core).
Axes of the slice: x: 4 (x_hi: 2, x_lo: 2; x = x_hi * 2 + x_lo), y: 4, z: 8, core: 2. Of those that a mesh axis runs over, the one named last changes fastest.
Arguments:
- psi: bfloat16 [32, 384, 384], P('sec'), may hold values from -6 to 6
- left_ops: bfloat16 [128, 32, 384, 384], P('opg', 'sec'), may hold values from -0.15625 to 0.15625
- right_ops: bfloat16 [128, 32, 384, 384], P('opg', 'sec'), may hold values from -0.109375 to 0.109375
- source: int32 [128, 32], P('opg', 'sec'), may hold values from 0 to 31
- coef_index: int32 [128, 32], P('opg', 'sec'), may hold values from 0 to 63
- sixj: float32 [64], replicated, may hold values from -1 to 1
Outputs:
- sigma: bfloat16 [384, 32, 384], P('opg', 'sec')
All inputs are finite; a program needn't handle non-finite values.
Results may differ from a plain program's by a relative error of at most 0.005.
Values may be sent and summed in bfloat16 or wider, within the bound.
A program may use at most 64 MiB of HBM per device.

v0:
```python
import jax
import jax.numpy as jnp
from jax import lax
from jax.sharding import PartitionSpec as P


def on_device(psi, left_ops, right_ops, source, coef_index, sixj):
    whole = lax.all_gather(psi, "sec", axis=0, tiled=True)
    picked = whole[source]
    table_ids = jnp.arange(sixj.shape[0], dtype=jnp.int32)
    onehot = (coef_index[:, :, None] == table_ids[None, None, :]).astype(jnp.float32)
    coef = jnp.sum(onehot * sixj[None, None, :], axis=-1)
    half = jnp.einsum(
        "psib,psbc->psic", left_ops, picked, preferred_element_type=jnp.float32
    ).astype(jnp.bfloat16)
    full = jnp.einsum("psic,psjc->psij", half, right_ops, preferred_element_type=jnp.float32)
    summed = jnp.sum(full * coef[:, :, None, None], axis=0)
    mine = lax.psum_scatter(
        jnp.transpose(summed, (1, 0, 2)), "opg", scatter_dimension=0, tiled=True
    )
    return mine.astype(jnp.bfloat16)


def solution(mesh):
    placed = (
        P("sec", None, None),
        P("opg", "sec", None, None),
        P("opg", "sec", None, None),
        P("opg", "sec"),
        P("opg", "sec"),
        P(),
    )
    return jax.shard_map(
        on_device, mesh=mesh, in_specs=placed, out_specs=P("opg", "sec", None), check_vma=False
    )
```

profile of v0, /device:TPU:4, one launch (start us, length us, event | category | flops | bytes accessed | tf_op | source)
XLA Modules:
  0.0 201.0 jit_solution(18159404103165478730)
XLA Ops:
  6.5 0.0 all-gather.2.cloned.1.call-start
  6.5 0.7 all-gather.2.cloned.1.call-update
  7.3 0.7 compare_select_fusion
  7.9 0.1 copy.16
  8.0 0.1 reshape.5
  8.1 0.9 select_reduce_fusion
  9.0 0.1 copy.19
  9.1 1.3 dynamic-slice
  11.0 82.1 %all-gather.2.cloned.1.call-done = bf16[32,384,384]{2,1,0:T(8,128)(2,1)} async-done(((bf16[2,384,384]{2,1,0:T(8,128)(2,1)}), bf16[32,384,384]{2,1,0:T(8,128)(2,1)}) %all-gather.2.cloned.1.call-update) | async-done | bytes 9437200 | tf_op jit(solution)/shard_map/all_gather | solution.py:8
  93.1 7.1 %gather_fusion = bf16[16,384,384]{2,1,0:T(8,128)(2,1)} fusion(bf16[32,384,384]{2,1,0:T(8,128)(2,1)} %all-gather.2.cloned.1.call-done, s32[1024]{0:T(1024)S(1)} %pad_clamp_fusion), kind=kCustom, calls=%fused_computation | custom fusion | bytes 9437248 | tf_op jit(solution)/shard_map/gather | solution.py:9
  100.2 9.9 %multiply_reduce_fusion = f32[2,384,384]{2,1,0:T(8,128)S(1)} fusion(f32[8,2]{1,0:T(8,128)S(1)} %copy.19, bf16[8,2,384,384]{3,2,1,0:T(8,128)(2,1)} %param.8, bf16[8,2,384,384]{3,2,1,0:T(8,128)(2,1)} %bitcast.6, bf16[8,2,384,384]{3,2,1,0:T(8,128)(2,1)} %param.7), kind=kOutput, calls=%fused_computation.1 | convolution fusion | flops 3630661632 | bytes 15335488 | tf_op jit(solution)/shard_map/psic,psjc->psij/dot_general | solution.py:16
  110.1 0.9 copy.20
  111.1 82.5 %all-reduce.2 = bf16[384,2,384]{2,1,0:T(2,128)(2,1)S(1)} all-reduce(f32[384,2,384]{2,1,0:T(2,128)S(1)} %copy.20), channel_id=2, replica_groups=mesh['opg'=16,'sec'=16] {'opg'}, use_global_device_ids=true, to_apply=%region_2.0.clone | all-reduce | flops 294912 | bytes 1769472
  193.5 0.7 dynamic-slice_convert_fusion
  (1 shorter events, 0.0 us)
Async XLA Ops:
  6.5 86.6 %all-gather.2.cloned.1.call-start = ((), (), s32[]{:S(2)}) async-start(), calls=%async_computation | async-start | bytes 10027008 | tf_op jit(solution)/shard_map/all_gather | solution.py:8
Sparse Core Ops, SparseCore 0:
  10.1 82.9 all-gather.1
where the time goes:
time: 201 us
  waiting for transfers between devices  82.8 us (41%)
  blocking collectives  82.5 us (41%)
  between operations  14.1 us (7%)
  local copies, waits for them, and re-layouts  10.2 us (5%)
  matrix products  9.89 us (5%)
    unnamed x1, blocking collectives  82.5 us
    all_gather x1, waiting for transfers between devices, on_device(): whole = lax.all_gather(psi, 'sec', axis=0, tiled=True)  82.1 us
    dot_general x1, matrix products, on_device(): jnp.einsum('psic,psjc->psij', half, right_ops, preferred_element_type=jnp...  9.89 us
    gather x1, local copies, waits for them, and re-layouts, on_device(): picked = whole[source]  7.13 us
  transfers between devices with their start and end apart: 1, of which 1 were waited for; matrix products, arithmetic and copies ran while one was open for 2% of the time, Pallas kernels for 0%

commit v1 on v0

v1 whole, which is shorter than its diff:
```python
import functools

import jax
import jax.numpy as jnp
from jax import lax
from jax.experimental import pallas as pl
from jax.experimental.pallas import tpu as pltpu
from jax.sharding import PartitionSpec as P

MESH = pl.DeviceIdType.MESH
SB = 384
CW = 128
NCH = SB // CW
NP = 8
ROWS = 24


class Place:
    def __init__(self):
        o, s = lax.axis_index("opg"), lax.axis_index("sec")
        self.z, self.xl = o // 2, o % 2
        self.xh, self.y, self.c = s // 8, (s // 2) % 4, s % 2
        self.colour = (self.xl + self.xh + self.z) % 2

    def at(self, z=None, xl=None, xh=None, y=None, c=None):
        z = self.z if z is None else z
        xl = self.xl if xl is None else xl
        xh = self.xh if xh is None else xh
        y = self.y if y is None else y
        c = self.c if c is None else c
        return (z * 2 + xl, (xh * 4 + y) * 2 + c)

    def neighbour(self, name):
        if name == "y+":
            return self.at(y=(self.y + 1) % 4)
        if name == "y-":
            return self.at(y=(self.y + 3) % 4)
        if name == "xc":
            return self.at(xl=1 - self.xl, xh=1 - self.xh)
        if name == "xp":
            return self.at(xl=1 - self.xl)
        if name == "z+":
            return self.at(z=(self.z + 1) % 8)
        if name == "z-":
            return self.at(z=(self.z + 7) % 8)
        assert name == "c"
        return self.at(c=1 - self.c)


def kernel(
    psi, left, right, source, coef_index, sixj, out,
    g0, g1, g2, lv, rv, hv, acc, sa, ra, sb, rb,
    load_sem, send_sem, recv_sem, rs_send, rs_recv,
):
    here = Place()
    gs = (g0, g1, g2)
    group = here.xh * 4 + here.y
    own = group * 4 + here.c * 2
    groups = {
        "O": group,
        "Y1": here.xh * 4 + (here.y + 1) % 4,
        "Y2": here.xh * 4 + (here.y + 2) % 4,
        "Y3": here.xh * 4 + (here.y + 3) % 4,
        "X0": (1 - here.xh) * 4 + here.y,
        "X1": (1 - here.xh) * 4 + (here.y + 1) % 4,
        "X2": (1 - here.xh) * 4 + (here.y + 2) % 4,
        "X3": (1 - here.xh) * 4 + (here.y + 3) % 4,
    }

    loads = [
        pltpu.make_async_copy(
            psi.at[:, :, pl.ds(k * CW, CW)], gs[k].at[pl.ds(own, 2)], load_sem.at[k]
        )
        for k in range(NCH)
    ]
    load_left = pltpu.make_async_copy(left, lv, load_sem.at[NCH])
    load_right = pltpu.make_async_copy(right, rv, load_sem.at[NCH + 1])
    for load in loads:
        load.start()
    load_left.start()
    load_right.start()

    barrier = pltpu.get_barrier_semaphore()
    near = [here.neighbour(n) for n in ("y+", "y-", "xc", "xp", "z+", "z-", "c")]
    far = [here.at(z=(here.z + d) % 8) for d in (2, 3, 4, 5, 6)]
    for device in near + far:
        pl.semaphore_signal(barrier, inc=1, device_id=device, device_id_type=MESH)
    pl.semaphore_wait(barrier, len(near) + len(far))

    slots = {}

    def message(k, name, to, who, lo, hi, both=False):
        slot = slots.setdefault(name, len(slots))
        if both:
            ref = gs[k].at[pl.ds(groups[who] * 4 + here.c * 2, 2)]
        else:
            ref = gs[k].at[groups[who] * 4 + here.c * 2 + here.colour, pl.ds(lo, hi - lo)]
        return pltpu.make_async_remote_copy(
            src_ref=ref,
            dst_ref=ref,
            send_sem=send_sem.at[k],
            recv_sem=recv_sem.at[k, slot],
            device_id=here.neighbour(to),
            device_id_type=MESH,
        )

    def send(k, name, to, who, lo=0, hi=SB, both=False):
        message(k, name, to, who, lo, hi, both).start()

    def recv(k, name, to, who, lo=0, hi=SB, both=False):
        message(k, name, to, who, lo, hi, both).wait_recv()

    PART = 320
    SWAP = {"Y1": "xp", "Y3": "z+", "X0": "z-", "Y2": "xp", "X1": "z+", "X3": "z-"}

    def swap(k, who):
        if who == "X2":
            for i, to in enumerate(("xp", "z+", "z-")):
                send(k, f"swap{who}{i}", to, who, i * 128, i * 128 + 128)
        else:
            send(k, f"swap{who}", SWAP[who], who)

    def swapped(k, who):
        if who == "X2":
            for i, to in enumerate(("xp", "z+", "z-")):
                recv(k, f"swap{who}{i}", to, who, i * 128, i * 128 + 128)
        else:
            recv(k, f"swap{who}", SWAP[who], who)
        send(k, f"core{who}", "c", who, both=True)

    def own_start(k):
        loads[k].wait()
        send(k, "Y3", "y+", "O")
        send(k, "Y1", "y-", "O")
        send(k, "X0", "xc", "O")
        send(k, "coreO", "c", "O", both=True)

    def got_y1(k):
        recv(k, "Y1", "y-", "O")
        send(k, "Y2b", "y-", "Y1", 192, SB)
        send(k, "X1b", "xc", "Y1", PART, SB)
        swap(k, "Y1")

    def got_y3(k):
        recv(k, "Y3", "y+", "O")
        send(k, "Y2a", "y+", "Y3", 0, 192)
        send(k, "X3b", "xc", "Y3", PART, SB)
        swap(k, "Y3")

    def got_x0(k):
        recv(k, "X0", "xc", "O")
        send(k, "X1a", "y-", "X0", 0, PART)
        send(k, "X3a", "y+", "X0", 0, PART)
        swap(k, "X0")

    def got_y2(k):
        recv(k, "Y2a", "y+", "Y3", 0, 192)
        send(k, "X2a", "xc", "Y2", 0, 192)
        recv(k, "Y2b", "y-", "Y1", 192, SB)
        send(k, "X2b", "xc", "Y2", 192, SB)
        swap(k, "Y2")

    def got_x1(k):
        recv(k, "X1a", "y-", "X0", 0, PART)
        recv(k, "X1b", "xc", "Y1", PART, SB)
        swap(k, "X1")

    def got_x3(k):
        recv(k, "X3a", "y+", "X0", 0, PART)
        recv(k, "X3b", "xc", "Y3", PART, SB)
        swap(k, "X3")

    def got_x2(k):
        recv(k, "X2a", "xc", "Y2", 0, 192)
        recv(k, "X2b", "xc", "Y2", 192, SB)
        swap(k, "X2")

    ALL = ("Y1", "Y3", "X0", "Y2", "X1", "X3", "X2")

    def gathered(k):
        for who in ("O",) + ALL:
            recv(k, f"core{who}", "c", who, both=True)

    def first(k, p, s):
        block = gs[k][source[p, s]]
        coef = sixj[coef_index[p, s]]
        half = jnp.dot(lv[p, s], block, preferred_element_type=jnp.float32)
        hv[s, p] = (half * coef).astype(jnp.bfloat16)

    def second(k, s):
        a = jnp.concatenate([hv[s, p] for p in range(NP)], axis=1)
        b = jnp.concatenate([rv[p, s, :, k * CW : (k + 1) * CW] for p in range(NP)], axis=1)
        part = lax.dot_general(
            a, b, (((1,), (1,)), ((), ())), preferred_element_type=jnp.float32
        ).reshape(8, 2, ROWS, SB)
        if k == 0:
            acc[s] = part
        else:
            acc[s] += part

    comm = [
        [
            functools.partial(own_start, k),
            functools.partial(got_y1, k),
            functools.partial(got_y3, k),
            functools.partial(got_x0, k),
            functools.partial(got_y2, k),
            functools.partial(got_x1, k),
            functools.partial(got_x3, k),
        ]
        + [functools.partial(swapped, k, w) for w in ALL[:3]]
        + [functools.partial(got_x2, k)]
        + [functools.partial(swapped, k, w) for w in ALL[3:]]
        + [functools.partial(gathered, k)]
        for k in range(NCH)
    ]
    work = [
        [
            step
            for s in range(2)
            for step in [functools.partial(first, k, p, s) for p in range(NP)]
            + [functools.partial(second, k, s)]
        ]
        for k in range(NCH)
    ]

    for k in range(NCH):
        steps = list(comm[k])
        todo = list(work[k - 1]) if k else []
        if k == 1:
            load_left.wait()
            load_right.wait()
        n, m = len(steps), len(todo)
        done = 0
        for i, step in enumerate(steps):
            step()
            upto = m * (i + 1) // n
            for task in todo[done:upto]:
                task()
            done = upto
    for task in work[NCH - 1]:
        task()

    mine, theirs = here.xl, 1 - here.xl
    order = (4, 3, 5, 2, 6, 1, 7, 0)
    pair = []
    for i, d in enumerate(order):
        z = (here.z + d) % 8
        sa[i] = jnp.concatenate([acc[0, z, theirs], acc[1, z, theirs]], axis=0).astype(jnp.bfloat16)
        copy = pltpu.make_async_remote_copy(
            src_ref=sa.at[i],
            dst_ref=ra.at[i],
            send_sem=rs_send.at[0],
            recv_sem=rs_recv.at[i],
            device_id=here.neighbour("xp"),
            device_id_type=MESH,
        )
        copy.start()
        pair.append(copy)
    total = None
    cross = []
    for i, d in enumerate(order):
        z = (here.z + d) % 8
        pair[i].wait_recv()
        both = jnp.concatenate([acc[0, z, mine], acc[1, z, mine]], axis=0) + ra[i].astype(jnp.float32)
        if d == 0:
            total = both
            continue
        sb[i] = both.astype(jnp.bfloat16)
        copy = pltpu.make_async_remote_copy(
            src_ref=sb.at[i],
            dst_ref=rb.at[i],
            send_sem=rs_send.at[1],
            recv_sem=rs_recv.at[8 + i],
            device_id=here.at(z=z),
            device_id_type=MESH,
        )
        copy.start()
        cross.append(copy)
    for i, copy in enumerate(cross):
        copy.wait_recv()
        total = total + rb[i].astype(jnp.float32)
    out[...] = total.astype(jnp.bfloat16)

    for k in range(NCH):
        ref = gs[k].at[pl.ds(0, 30)]
        pltpu.make_async_copy(ref, ref, send_sem.at[k]).wait()
    pltpu.make_async_copy(sa, sa, rs_send.at[0]).wait()
    pltpu.make_async_copy(sb, sb, rs_send.at[1]).wait()


def on_device(psi, left_ops, right_ops, source, coef_index, sixj):
    anywhere = pl.BlockSpec(memory_space=pl.ANY)
    scalars = pl.BlockSpec(memory_space=pltpu.SMEM)
    bf16, f32 = jnp.bfloat16, jnp.float32
    mine = pl.pallas_call(
        kernel,
        name="sigma",
        out_shape=jax.ShapeDtypeStruct((2 * ROWS, SB), bf16),
        in_specs=[anywhere] * 3 + [scalars] * 3,
        out_specs=pl.BlockSpec(memory_space=pltpu.VMEM),
        scratch_shapes=[pltpu.VMEM((32, SB, CW), bf16)] * NCH
        + [
            pltpu.VMEM((NP, 2, SB, SB), bf16),
            pltpu.VMEM((NP, 2, SB, SB), bf16),
            pltpu.VMEM((2, NP, SB, CW), bf16),
            pltpu.VMEM((2, 8, 2, ROWS, SB), f32),
            pltpu.VMEM((8, 2 * ROWS, SB), bf16),
            pltpu.VMEM((8, 2 * ROWS, SB), bf16),
            pltpu.VMEM((7, 2 * ROWS, SB), bf16),
            pltpu.VMEM((7, 2 * ROWS, SB), bf16),
            pltpu.SemaphoreType.DMA((NCH + 2,)),
            pltpu.SemaphoreType.DMA((NCH,)),
            pltpu.SemaphoreType.DMA((NCH, 28)),
            pltpu.SemaphoreType.DMA((2,)),
            pltpu.SemaphoreType.DMA((15,)),
        ],
        compiler_params=pltpu.CompilerParams(
            collective_id=0, has_side_effects=True, vmem_limit_bytes=48 * 2**20
        ),
    )(psi, left_ops, right_ops, source, coef_index, sixj)
    return jnp.transpose(mine.reshape(2, ROWS, SB), (1, 0, 2))


def solution(mesh):
    placed = (
        P("sec", None, None),
        P("opg", "sec", None, None),
        P("opg", "sec", None, None),
        P("opg", "sec"),
        P("opg", "sec"),
        P(),
    )
    return jax.shard_map(
        on_device, mesh=mesh, in_specs=placed, out_specs=P("opg", "sec", None), check_vma=False
    )
```

time: 201 us -> 83.7 us (0.42)
  the two profiles are of different devices: /device:TPU:4 before, /device:TPU:1 now
where the time goes in v1:
time: 83.7 us; the launch traced here: 83.5 us
  Pallas kernels  77.3 us (92%)
  local copies, waits for them, and re-layouts  6.21 us (7%)
    pallas_call x1, Pallas kernels, on_device(): pl.pallas_call(kernel, name='sigma', out_shape=jax.ShapeDtypeStruct((2 *...  77.3 us
    unnamed x8, local copies, waits for them, and re-layouts  5.56 us

profile of v1, /device:TPU:1, one launch (start us, length us, event | category | flops | bytes accessed | tf_op | source)
XLA Modules:
  0.0 83.5 jit_solution(13841557077487790501)
XLA Ops:
  0.0 0.8 copy.7.source
  0.8 0.8 copy.8.coef_index
  1.5 0.0 copy-start
  1.5 2.3 %copy-done = bf16[8,2,384,384]{3,2,1,0:T(8,128)(2,1)S(1)} copy-done((bf16[8,2,384,384]{3,2,1,0:T(8,128)(2,1)S(1)}, bf16[8,2,384,384]{3,2,1,0:T(8,128)(2,1)}, u32[]{:S(2)}) %copy-start) | copy-done | bytes 4718616
  3.8 0.0 copy-start.1
  3.8 1.1 %copy-done.1 = bf16[2,384,384]{2,1,0:T(8,128)(2,1)S(1)} copy-done((bf16[2,384,384]{2,1,0:T(8,128)(2,1)S(1)}, bf16[2,384,384]{2,1,0:T(8,128)(2,1)}, u32[]{:S(2)}) %copy-start.1) | copy-done | bytes 589848
  4.9 0.0 copy-start.2
  4.9 0.7 copy-done.2
  5.6 77.3 %sigma.1 = bf16[48,384]{1,0:T(8,128)(2,1)S(1)} custom-call(bf16[2,384,384]{2,1,0:T(8,128)(2,1)S(1)} %copy-done.1, bf16[8,2,384,384]{3,2,1,0:T(8,128)(2,1)S(1)} %copy-done, bf16[8,2,384,384]{3,2,1,0:T(8,128)(2,1)} %right.1, s32[8,2]{1,0:T(8,128)S(1)} %copy.7.source, s32[8,2]{1,0:T(8,128)S(1)} %copy.8.coef_index, f32[64]{0:T(128)S(1)} %copy-done.2), custom_call_target="tpu_custom_call" | custom-call | tf_op jit(solution)/shard_map/sigma/pallas_call | solution.py:296
  82.8 0.6 copy.11
Async XLA Ops:
  1.5 2.3 %copy-start = (bf16[8,2,384,384]{3,2,1,0:T(8,128)(2,1)S(1)}, bf16[8,2,384,384]{3,2,1,0:T(8,128)(2,1)}, u32[]{:S(2)}) copy-start(bf16[8,2,384,384]{3,2,1,0:T(8,128)(2,1)} %left.1) | copy-start | bytes 14155780
  3.8 1.1 %copy-start.1 = (bf16[2,384,384]{2,1,0:T(8,128)(2,1)S(1)}, bf16[2,384,384]{2,1,0:T(8,128)(2,1)}, u32[]{:S(2)}) copy-start(bf16[2,384,384]{2,1,0:T(8,128)(2,1)} %psi.1) | copy-start | bytes 1769476
  4.9 0.7 copy-start.2

commit v2 on v0

v2 whole, which is shorter than its diff:
```python
import functools

import jax
import jax.numpy as jnp
from jax import lax
from jax.experimental import pallas as pl
from jax.experimental.pallas import tpu as pltpu
from jax.sharding import PartitionSpec as P

MESH = pl.DeviceIdType.MESH
SB = 384
WIDTHS = (1, 2)
NCH = len(WIDTHS)
COLS = [slice(128 * sum(WIDTHS[:k]), 128 * sum(WIDTHS[: k + 1])) for k in range(NCH)]
NP = 8
ROWS = 24


YP, YM, XC, XP, ZP, ZM, CORE, XPC, ZPC, ZMC = LINKS = range(10)
OWN, Y1, Y2, Y3, X0, X1, X2, X3 = range(8)
READY, WORK = -1, -2
MINE, OTHER, BOTH = range(3)
MESSAGES = (
    (
        (YM, OWN, 0, 384, MINE, ()),
        (YP, OWN, 0, 384, MINE, ()),
        (XC, OWN, 0, 384, MINE, ()),
        (YP, Y3, 0, 192, MINE, (1,)),
        (YM, Y1, 192, 384, MINE, (0,)),
        (YM, X0, 0, 320, MINE, (2,)),
        (YP, X0, 0, 320, MINE, (2,)),
        (XC, Y1, 320, 384, MINE, (0,)),
        (XC, Y3, 320, 384, MINE, (1,)),
        (XC, Y2, 0, 192, MINE, (3,)),
        (XC, Y2, 192, 384, MINE, (4,)),
        (ZM, Y1, 0, 384, MINE, (0,)),
        (XP, Y3, 0, 384, MINE, (1,)),
        (ZP, X0, 0, 384, MINE, (2,)),
        (XP, Y2, 0, 128, MINE, (3,)),
        (ZP, Y2, 128, 256, MINE, (3, 4)),
        (ZM, Y2, 256, 384, MINE, (4,)),
        (XP, X1, 0, 128, MINE, (5,)),
        (ZP, X1, 128, 256, MINE, (5,)),
        (ZM, X1, 256, 384, MINE, (5, 7)),
        (XP, X3, 0, 128, MINE, (6,)),
        (ZP, X3, 128, 256, MINE, (6,)),
        (ZM, X3, 256, 384, MINE, (6, 8)),
        (XP, X2, 0, 128, MINE, (9,)),
        (ZP, X2, 128, 256, MINE, (9, 10)),
        (ZM, X2, 256, 384, MINE, (10,)),
        (CORE, OWN, 0, 384, BOTH, ()),
        (CORE, Y1, 0, 384, BOTH, (0, 11)),
        (CORE, Y3, 0, 384, BOTH, (1, 12)),
        (CORE, X0, 0, 384, BOTH, (2, 13)),
        (CORE, Y2, 0, 384, BOTH, (3, 4, 14, 15, 16)),
        (CORE, X1, 0, 384, BOTH, (5, 7, 17, 18, 19)),
        (CORE, X3, 0, 384, BOTH, (6, 8, 20, 21, 22)),
        (CORE, X2, 0, 384, BOTH, (9, 10, 23, 24, 25)),
    ),
    (
        (YM, OWN, 0, 192, MINE, ()),
        (YM, OWN, 192, 384, MINE, ()),
        (YP, OWN, 0, 192, MINE, ()),
        (YP, OWN, 192, 384, MINE, ()),
        (XC, OWN, 0, 192, MINE, ()),
        (XC, OWN, 192, 384, MINE, ()),
        (YP, Y3, 0, 192, MINE, (2,)),
        (YM, Y1, 192, 384, MINE, (1,)),
        (YM, X0, 0, 128, MINE, (4,)),
        (YM, X0, 128, 256, MINE, (4, 5)),
        (YP, X0, 0, 128, MINE, (4,)),
        (YP, X0, 128, 256, MINE, (4, 5)),
        (XC, Y1, 256, 384, MINE, (1,)),
        (XC, Y3, 256, 384, MINE, (3,)),
        (YM, X1, 0, 64, MINE, (8,)),
        (YP, X3, 320, 384, MINE, (13,)),
        (XC, Y2, 64, 192, MINE, (6,)),
        (XC, Y2, 192, 320, MINE, (7,)),
        (XP, Y1, 0, 128, MINE, (0,)),
        (XP, Y1, 128, 256, MINE, (0, 1)),
        (XP, Y1, 256, 384, MINE, (1,)),
        (ZM, Y3, 0, 192, MINE, (2,)),
        (ZM, Y3, 192, 384, MINE, (3,)),
        (ZP, X0, 0, 192, MINE, (4,)),
        (ZP, X0, 192, 384, MINE, (5,)),
        (ZM, Y2, 0, 192, MINE, (6,)),
        (ZM, Y2, 192, 384, MINE, (7,)),
        (ZP, X1, 0, 128, MINE, (8,)),
        (ZP, X1, 128, 256, MINE, (9,)),
        (ZP, X1, 256, 384, MINE, (12,)),
        (XP, X3, 0, 128, MINE, (10,)),
        (XP, X3, 128, 256, MINE, (11,)),
        (XP, X3, 256, 384, MINE, (13,)),
        (XP, X2, 0, 128, MINE, (14, 16)),
        (XPC, X2, 0, 128, MINE, (14, 16)),
        (ZP, X2, 128, 256, MINE, (16, 17)),
        (ZPC, X2, 128, 256, MINE, (16, 17)),
        (ZM, X2, 256, 384, MINE, (15, 17)),
        (ZMC, X2, 256, 384, MINE, (15, 17)),
        (CORE, OWN, 0, 384, BOTH, ()),
        (CORE, Y1, 0, 384, BOTH, (0, 1, 18, 19, 20)),
        (CORE, Y3, 0, 384, BOTH, (2, 3, 21, 22)),
        (CORE, X0, 0, 384, BOTH, (4, 5, 23, 24)),
        (CORE, Y2, 0, 384, BOTH, (6, 7, 25, 26)),
        (CORE, X1, 0, 384, BOTH, (8, 9, 12, 27, 28, 29)),
        (CORE, X3, 0, 384, MINE, (10, 11, 13)),
        (CORE, X3, 0, 384, OTHER, (30, 31, 32)),
        (CORE, X2, 0, 384, MINE, (14, 15, 16, 17)),
    ),
)
ORDER = (
    (0, 0), (0, 1), (1, 5), (0, 26), (1, 39), (1, 1), (1, 2), (0, 2), (1, 0), (1, 3), (1, 4),
    (0, 11), (0, 12), (1, 24), (0, 4), (0, 3), (0, 7), (0, 8), (1, 20), (1, 21), (0, 13), (1, 6),
    (0, 5), (1, 12), (1, 7), (1, 19), (1, 22), (1, 23), (0, 6), (1, 13), (0, 28), (0, 27), (1, 18),
    (0, 10), (0, 16), (0, 15), (1, 8), (1, 10), (0, 9), (0, 14), (1, 29), (0, 29), (0, 19), (0, 17),
    (1, 25), (1, 16), (1, 9), (1, 11), (0, 18), (1, 32), (1, 41), (1, 42), (1, 15), (1, 17),
    (0, 21), (0, 22), (1, 40), (0, 20), (0, 25), (0, 30), (0, 23), (0, 24), (1, 14), (1, 27),
    (1, 26), (1, 30), (0, 31), (1, 45), (1, 28), (1, 31), (0, 32), (1, 37), (1, 36), (1, 47),
    (1, 34), (0, 33), (1, 38), (1, 35), (1, 33), (1, 43), (READY, 0), (WORK, 1), (1, 44), (1, 46),
    (WORK, 17), (READY, 1),
)
FIRST, *_, LAST = [k for what, k in ORDER if what == READY]

DIRECT = ()
FAR, NEAR = (4, 5, 6, 7), (3, 2, 1)
FINISH = (4, 5, 6, 7, 0, 3, 2, 1)


class Place:
    def __init__(self):
        o, s = lax.axis_index("opg"), lax.axis_index("sec")
        self.z, self.xl = o // 2, o % 2
        self.xh, self.y, self.c = s // 8, (s // 2) % 4, s % 2
        self.colour = (self.xl + self.xh + self.z) % 2

    def at(self, z=None, xl=None, xh=None, y=None, c=None):
        z = self.z if z is None else z
        xl = self.xl if xl is None else xl
        xh = self.xh if xh is None else xh
        y = self.y if y is None else y
        c = self.c if c is None else c
        return (z * 2 + xl, (xh * 4 + y) * 2 + c)

    def neighbour(self, link):
        if link == YP:
            return self.at(y=(self.y + 1) % 4)
        if link == YM:
            return self.at(y=(self.y + 3) % 4)
        if link == XC:
            return self.at(xl=1 - self.xl, xh=1 - self.xh)
        if link == XP:
            return self.at(xl=1 - self.xl)
        if link == ZP:
            return self.at(z=(self.z + 1) % 8)
        if link == ZM:
            return self.at(z=(self.z + 7) % 8)
        if link == CORE:
            return self.at(c=1 - self.c)
        if link == XPC:
            return self.at(xl=1 - self.xl, c=1 - self.c)
        if link == ZPC:
            return self.at(z=(self.z + 1) % 8, c=1 - self.c)
        assert link == ZMC
        return self.at(z=(self.z + 7) % 8, c=1 - self.c)


def kernel(
    psi, left, right, source_in, coef_index_in, sixj_in, out, gs, source, coef_index, sixj,
    lv, rv, hv, acc, sa, ra, sb, rb, sd, rd, load_sem, send_sem, recv_sem, rs_send, rs_recv,
):
    here = Place()
    group = here.xh * 4 + here.y
    own = group * 4 + here.c * 2
    groups = [x * 4 + (here.y + d) % 4 for x in (here.xh, 1 - here.xh) for d in range(4)]

    loads = [
        pltpu.make_async_copy(
            psi.at[:, :, COLS[k]], gs[k].at[pl.ds(own, 2)], load_sem.at[k]
        )
        for k in range(NCH)
    ]
    tables = [
        pltpu.make_async_copy(source_in, source, load_sem.at[NCH + 2]),
        pltpu.make_async_copy(coef_index_in, coef_index, load_sem.at[NCH + 3]),
        pltpu.make_async_copy(sixj_in, sixj, load_sem.at[NCH + 4]),
    ]
    load_left = pltpu.make_async_copy(left, lv, load_sem.at[NCH])
    load_right = pltpu.make_async_copy(right, rv, load_sem.at[NCH + 1])
    for load in loads:
        load.start()

    barrier = pltpu.get_barrier_semaphore()
    adjacent = [here.neighbour(n) for n in LINKS]
    for device in adjacent:
        pl.semaphore_signal(barrier, inc=1, device_id=device, device_id_type=MESH)
    pl.semaphore_wait(barrier, len(adjacent))

    def message(k, i):
        link, who, lo, hi, sector, _ = MESSAGES[k][i]
        first = groups[who] * 4 + here.c * 2
        if sector == BOTH:
            ref = gs[k].at[pl.ds(first, 2)]
        else:
            sector = first + (here.colour if sector == MINE else 1 - here.colour)
            ref = gs[k].at[sector, pl.ds(lo, hi - lo)]
        return pltpu.make_async_remote_copy(
            src_ref=ref,
            dst_ref=ref,
            send_sem=send_sem.at[k],
            recv_sem=recv_sem.at[k, i],
            device_id=here.neighbour(link),
            device_id_type=MESH,
        )

    arrived = set()

    def arrival(k, i):
        if (k, i) not in arrived:
            arrived.add((k, i))
            message(k, i).wait_recv()

    def first(k, p, s, rows=slice(0, SB)):
        half = jnp.dot(lv[p, s, rows], gs[k][source[s, p]], preferred_element_type=jnp.float32)
        if WIDTHS[k] == 1:
            half = half * sixj[coef_index[s, p]]
        hv[s, p, rows, : 128 * WIDTHS[k]] = half.astype(jnp.bfloat16)

    def times_transposed(a, b):
        return lax.dot_general(a, b, (((1,), (1,)), ((), ())), preferred_element_type=jnp.float32)

    def second(k, s, rows=slice(0, SB), zs=slice(0, 8)):
        halves = [hv[s, p, rows, : 128 * WIDTHS[k]] for p in range(NP)]
        rights = [rv[p, s, :, COLS[k]] for p in range(NP)]
        if WIDTHS[k] == 1:
            part = times_transposed(jnp.concatenate(halves, axis=1), jnp.concatenate(rights, axis=1))
        else:
            part = sum(
                times_transposed(halves[p], rights[p]) * sixj[coef_index[s, p]] for p in range(NP)
            )
        part = part.reshape(-1, 2, ROWS, SB)
        if k == FIRST:
            acc[s, zs] = part
        else:
            acc[s, zs] += part

    mine, theirs = here.xl, 1 - here.xl
    near, low = here.z // 4, here.z % 4
    flips = (low, low + 1 - 2 * (low % 2), (low + 2) % 4, 3 - low)
    places = [4 * near + flips[m] for m in range(4)]
    places += [4 * (1 - near) + flips[m] for m in range(4)]

    def partial_sum(m, whose):
        return jnp.concatenate([acc[s, places[m], whose] for s in range(2)], axis=0)

    def to_partner(m):
        return pltpu.make_async_remote_copy(
            src_ref=sa.at[m],
            dst_ref=ra.at[m],
            send_sem=rs_send.at[0],
            recv_sem=rs_recv.at[m],
            device_id=here.neighbour(XP),
            device_id_type=MESH,
        )

    def along_z(m):
        src, dst = (sd, rd) if m in DIRECT else (sb, rb)
        slot = DIRECT.index(m) if m in DIRECT else m - 1
        return pltpu.make_async_remote_copy(
            src_ref=src.at[slot],
            dst_ref=dst.at[slot],
            send_sem=rs_send.at[2 if m in DIRECT else 1],
            recv_sem=rs_recv.at[8 + m],
            device_id=here.at(z=places[m]),
            device_id_type=MESH,
        )

    def share(m):
        if m in DIRECT:
            both = jnp.concatenate([partial_sum(m, mine), partial_sum(m, theirs)], axis=0)
            sd[DIRECT.index(m)] = both.astype(jnp.bfloat16)
            along_z(m).start()
        else:
            sa[m] = partial_sum(m, theirs).astype(jnp.bfloat16)
            to_partner(m).start()

    def last_tasks(k):
        tasks = []
        for half, ms in ((1 - near, FAR), (near, NEAR)):
            rows = pl.ds(pl.multiple_of(half * (SB // 2), SB // 2), SB // 2)
            zs = pl.ds(half * 4, 4)
            for s in range(2):
                tasks += [functools.partial(first, k, p, s, rows) for p in range(NP)]
                tasks.append(functools.partial(second, k, s, rows, zs))
            tasks += [functools.partial(share, m) for m in ms]
        return tasks

    todo = []
    loaded = set()
    for k, what in ORDER:
        if k == READY:
            if what == FIRST:
                for load in (load_left, load_right, *tables):
                    load.wait()
            for i in range(len(MESSAGES[what])):
                arrival(what, i)
            if what == LAST:
                todo += last_tasks(what)
            else:
                for s in range(2):
                    todo += [functools.partial(first, what, p, s) for p in range(NP)]
                    todo.append(functools.partial(second, what, s))
        elif k == WORK:
            for task in todo[:what]:
                task()
            todo = todo[what:]
        else:
            if k not in loaded:
                loaded.add(k)
                loads[k].wait()
                if len(loaded) == NCH:
                    for load in (load_left, load_right, *tables):
                        load.start()
            for i in MESSAGES[k][what][5]:
                arrival(k, i)
            message(k, what).start()

    for task in todo:
        task()

    total = None
    for m in FINISH:
        if m == 0:
            total = partial_sum(0, mine)
            gift = partial_sum(0, theirs)
            for n in DIRECT:
                along_z(n).wait_recv()
                total = total + rd[DIRECT.index(n), : 2 * ROWS].astype(jnp.float32)
                gift = gift + rd[DIRECT.index(n), 2 * ROWS :].astype(jnp.float32)
            sa[0] = gift.astype(jnp.bfloat16)
            to_partner(0).start()
        else:
            to_partner(m).wait_recv()
            sb[m - 1] = (partial_sum(m, mine) + ra[m].astype(jnp.float32)).astype(jnp.bfloat16)
            along_z(m).start()
    for m in FINISH:
        if m == 0:
            to_partner(0).wait_recv()
            total = total + ra[0].astype(jnp.float32)
        else:
            along_z(m).wait_recv()
            total = total + rb[m - 1].astype(jnp.float32)
    out[...] = total.astype(jnp.bfloat16)

    for k in range(NCH):
        rows = sum((hi - lo) * (2 if sector == BOTH else 1) for _, _, lo, hi, sector, _ in MESSAGES[k])
        assert rows % SB == 0
        ref = gs[k].at[pl.ds(0, rows // SB)]
        pltpu.make_async_copy(ref, ref, send_sem.at[k]).wait()
    sent = [(sa.at[pl.ds(0, 8 - len(DIRECT))], 0), (sb.at[pl.ds(0, 7 - len(DIRECT))], 1)]
    if DIRECT:
        sent.append((sd, 2))
    for ref, i in sent:
        pltpu.make_async_copy(ref, ref, rs_send.at[i]).wait()


def on_device(psi, left_ops, right_ops, source, coef_index, sixj):
    hbm = pl.BlockSpec(memory_space=pltpu.HBM)
    bf16, f32 = jnp.bfloat16, jnp.float32
    mine = pl.pallas_call(
        kernel,
        name="sigma",
        out_shape=jax.ShapeDtypeStruct((2 * ROWS, SB), bf16),
        in_specs=[hbm] * 6,
        out_specs=pl.BlockSpec(memory_space=pltpu.VMEM),
        scratch_shapes=[
            [pltpu.VMEM((32, SB, 128 * w), bf16) for w in WIDTHS],
            pltpu.SMEM((2, NP), jnp.int32),
            pltpu.SMEM((2, NP), jnp.int32),
            pltpu.SMEM((64,), f32),
            pltpu.VMEM((NP, 2, SB, SB), bf16),
            pltpu.VMEM((NP, 2, SB, SB), bf16),
            pltpu.VMEM((2, NP, SB, 128 * max(WIDTHS)), bf16),
            pltpu.VMEM((2, 8, 2, ROWS, SB), f32),
            pltpu.VMEM((8, 2 * ROWS, SB), bf16),
            pltpu.VMEM((8, 2 * ROWS, SB), bf16),
            pltpu.VMEM((7, 2 * ROWS, SB), bf16),
            pltpu.VMEM((7, 2 * ROWS, SB), bf16),
            pltpu.VMEM((max(1, len(DIRECT)), 4 * ROWS, SB), bf16),
            pltpu.VMEM((max(1, len(DIRECT)), 4 * ROWS, SB), bf16),
            pltpu.SemaphoreType.DMA((NCH + 5,)),
            pltpu.SemaphoreType.DMA((NCH,)),
            pltpu.SemaphoreType.DMA((NCH, max(len(table) for table in MESSAGES))),
            pltpu.SemaphoreType.DMA((3,)),
            pltpu.SemaphoreType.DMA((16,)),
        ],
        compiler_params=pltpu.CompilerParams(
            collective_id=0, has_side_effects=True, vmem_limit_bytes=56 * 2**20
        ),
    )(psi, left_ops, right_ops, source.T, coef_index.T, sixj)
    return jnp.transpose(mine.reshape(2, ROWS, SB), (1, 0, 2))


def solution(mesh):
    placed = (
        P("sec", None, None),
        P("opg", "sec", None, None),
        P("opg", "sec", None, None),
        P("opg", "sec"),
        P("opg", "sec"),
        P(),
    )
    return jax.shard_map(
        on_device, mesh=mesh, in_specs=placed, out_specs=P("opg", "sec", None), check_vma=False
    )
```

time: 201 us -> 49.6 us (0.25)
  the two profiles are of different devices: /device:TPU:4 before, /device:TPU:1 now
where the time goes in v2:
time: 49.6 us; the launch traced here: 49.4 us
  Pallas kernels  48 us (97%)
  local copies, waits for them, and re-layouts  1.41 us (3%)
    pallas_call x1, Pallas kernels, on_device(): pl.pallas_call(kernel, name='sigma', out_shape=jax.ShapeDtypeStruct((2 *...  48 us
    reshape x1, local copies, waits for them, and re-layouts, on_device(): return jnp.transpose(mine.reshape(2, ROWS, SB), (1, 0, 2))  1.41 us

profile of v2, /device:TPU:1, one launch (start us, length us, event | category | flops | bytes accessed | tf_op | source)
XLA Modules:
  0.0 49.4 jit_solution(5418680036733315974)
XLA Ops:
  0.0 48.0 %sigma.1 = bf16[48,384]{1,0:T(8,128)(2,1)} custom-call(bf16[2,384,384]{2,1,0:T(8,128)(2,1)} %psi.1, bf16[8,2,384,384]{3,2,1,0:T(8,128)(2,1)} %left.1, bf16[8,2,384,384]{3,2,1,0:T(8,128)(2,1)} %right.1, s32[2,8]{1,0:T(2,128)} %bitcast.7, s32[2,8]{1,0:T(2,128)} %bitcast.8, f32[64]{0:T(128)} %sixj_in.1), custom_call_target="tpu_custom_call" | custom-call | tf_op jit(solution)/shard_map/sigma/pallas_call | solution.py:369
  48.0 1.4 %copy.9 = bf16[2,24,384]{2,0,1:T(2,128)(2,1)} copy(bf16[2,24,384]{2,1,0:T(8,128)(2,1)} %bitcast.6) | data formatting | bytes 73728 | tf_op jit(solution)/shard_map/reshape | solution.py:400

commit v3 on v2

--- a/solution.py
+++ b/solution.py
@@ -22,109 +22,106 @@
 MINE, OTHER, BOTH = range(3)
 MESSAGES = (
     (
-        (YM, OWN, 0, 384, MINE, ()),
-        (YP, OWN, 0, 384, MINE, ()),
+        (YM, OWN, 0, 128, MINE, ()),
+        (YM, OWN, 128, 384, MINE, ()),
+        (YP, OWN, 0, 128, MINE, ()),
+        (YP, OWN, 128, 384, MINE, ()),
         (XC, OWN, 0, 384, MINE, ()),
-        (YP, Y3, 0, 192, MINE, (1,)),
-        (YM, Y1, 192, 384, MINE, (0,)),
-        (YM, X0, 0, 320, MINE, (2,)),
-        (YP, X0, 0, 320, MINE, (2,)),
-        (XC, Y1, 320, 384, MINE, (0,)),
-        (XC, Y3, 320, 384, MINE, (1,)),
-        (XC, Y2, 0, 192, MINE, (3,)),
-        (XC, Y2, 192, 384, MINE, (4,)),
-        (ZM, Y1, 0, 384, MINE, (0,)),
-        (XP, Y3, 0, 384, MINE, (1,)),
-        (ZP, X0, 0, 384, MINE, (2,)),
-        (XP, Y2, 0, 128, MINE, (3,)),
-        (ZP, Y2, 128, 256, MINE, (3, 4)),
-        (ZM, Y2, 256, 384, MINE, (4,)),
-        (XP, X1, 0, 128, MINE, (5,)),
-        (ZP, X1, 128, 256, MINE, (5,)),
-        (ZM, X1, 256, 384, MINE, (5, 7)),
-        (XP, X3, 0, 128, MINE, (6,)),
-        (ZP, X3, 128, 256, MINE, (6,)),
-        (ZM, X3, 256, 384, MINE, (6, 8)),
-        (XP, X2, 0, 128, MINE, (9,)),
-        (ZP, X2, 128, 256, MINE, (9, 10)),
-        (ZM, X2, 256, 384, MINE, (10,)),
+        (YP, Y3, 0, 192, MINE, (2, 3)),
+        (YM, Y1, 192, 384, MINE, (1,)),
+        (YM, X0, 0, 192, MINE, (4,)),
+        (YM, X0, 192, 320, MINE, (4,)),
+        (YP, X0, 0, 192, MINE, (4,)),
+        (YP, X0, 192, 320, MINE, (4,)),
+        (XC, Y1, 320, 384, MINE, (1,)),
+        (XC, Y3, 320, 384, MINE, (3,)),
+        (XC, Y2, 0, 192, MINE, (5,)),
+        (XC, Y2, 192, 384, MINE, (6,)),
+        (ZM, Y1, 0, 384, MINE, (0, 1)),
+        (ZP, Y3, 0, 384, MINE, (2, 3)),
+        (XP, X0, 0, 384, MINE, (4,)),
+        (ZP, Y2, 0, 384, MINE, (5, 6)),
+        (XP, X1, 0, 384, MINE, (7, 8, 11)),
+        (ZM, X3, 0, 192, MINE, (9,)),
+        (ZM, X3, 192, 384, MINE, (10, 12)),
+        (ZP, X2, 0, 128, MINE, (13,)),
+        (XP, X2, 128, 256, MINE, (13, 14)),
+        (ZM, X2, 256, 384, MINE, (14,)),
         (CORE, OWN, 0, 384, BOTH, ()),
-        (CORE, Y1, 0, 384, BOTH, (0, 11)),
-        (CORE, Y3, 0, 384, BOTH, (1, 12)),
-        (CORE, X0, 0, 384, BOTH, (2, 13)),
-        (CORE, Y2, 0, 384, BOTH, (3, 4, 14, 15, 16)),
-        (CORE, X1, 0, 384, BOTH, (5, 7, 17, 18, 19)),
-        (CORE, X3, 0, 384, BOTH, (6, 8, 20, 21, 22)),
-        (CORE, X2, 0, 384, BOTH, (9, 10, 23, 24, 25)),
+        (CORE, Y1, 0, 384, BOTH, (0, 1, 15)),
+        (CORE, Y3, 0, 384, BOTH, (2, 3, 16)),
+        (CORE, X0, 0, 384, BOTH, (4, 17)),
+        (CORE, Y2, 0, 384, BOTH, (5, 6, 18)),
+        (CORE, X1, 0, 384, BOTH, (7, 8, 11, 19)),
+        (CORE, X3, 0, 384, BOTH, (9, 10, 12, 20, 21)),
+        (CORE, X2, 0, 384, BOTH, (13, 14, 22, 23, 24)),
     ),
     (
         (YM, OWN, 0, 192, MINE, ()),
         (YM, OWN, 192, 384, MINE, ()),
         (YP, OWN, 0, 192, MINE, ()),
         (YP, OWN, 192, 384, MINE, ()),
-        (XC, OWN, 0, 192, MINE, ()),
-        (XC, OWN, 192, 384, MINE, ()),
-        (YP, Y3, 0, 192, MINE, (2,)),
+        (XC, OWN, 0, 64, MINE, ()),
+        (XC, OWN, 64, 384, MINE, ()),
+        (YP, Y3, 0, 64, MINE, (2,)),
+        (YP, Y3, 64, 192, MINE, (2,)),
         (YM, Y1, 192, 384, MINE, (1,)),
-        (YM, X0, 0, 128, MINE, (4,)),
-        (YM, X0, 128, 256, MINE, (4, 5)),
-        (YP, X0, 0, 128, MINE, (4,)),
-        (YP, X0, 128, 256, MINE, (4, 5)),
-        (XC, Y1, 256, 384, MINE, (1,)),
-        (XC, Y3, 256, 384, MINE, (3,)),
-        (YM, X1, 0, 64, MINE, (8,)),
-        (YP, X3, 320, 384, MINE, (13,)),
-        (XC, Y2, 64, 192, MINE, (6,)),
-        (XC, Y2, 192, 320, MINE, (7,)),
-        (XP, Y1, 0, 128, MINE, (0,)),
-        (XP, Y1, 128, 256, MINE, (0, 1)),
-        (XP, Y1, 256, 384, MINE, (1,)),
-        (ZM, Y3, 0, 192, MINE, (2,)),
+        (YM, X0, 0, 64, MINE, (4,)),
+        (YM, X0, 64, 192, MINE, (5,)),
+        (YP, X0, 0, 64, MINE, (4,)),
+        (YP, X0, 64, 192, MINE, (5,)),
+        (XC, Y1, 192, 384, MINE, (1,)),
+        (XC, Y3, 192, 384, MINE, (3,)),
+        (YM, X1, 0, 64, MINE, (9,)),
+        (YM, X1, 64, 128, MINE, (10,)),
+        (YP, X3, 256, 384, MINE, (14,)),
+        (XC, Y2, 128, 192, MINE, (7,)),
+        (XC, Y2, 192, 256, MINE, (8,)),
+        (YM, OWN, 0, 192, OTHER, ()),
+        (YP, OWN, 0, 192, OTHER, ()),
+        (XC, OWN, 0, 64, OTHER, ()),
+        (ZP, Y1, 192, 384, MINE, (1,)),
         (ZM, Y3, 192, 384, MINE, (3,)),
-        (ZP, X0, 0, 192, MINE, (4,)),
-        (ZP, X0, 192, 384, MINE, (5,)),
-        (ZM, Y2, 0, 192, MINE, (6,)),
-        (ZM, Y2, 192, 384, MINE, (7,)),
-        (ZP, X1, 0, 128, MINE, (8,)),
-        (ZP, X1, 128, 256, MINE, (9,)),
-        (ZP, X1, 256, 384, MINE, (12,)),
-        (XP, X3, 0, 128, MINE, (10,)),
-        (XP, X3, 128, 256, MINE, (11,)),
-        (XP, X3, 256, 384, MINE, (13,)),
-        (XP, X2, 0, 128, MINE, (14, 16)),
-        (XPC, X2, 0, 128, MINE, (14, 16)),
-        (ZP, X2, 128, 256, MINE, (16, 17)),
-        (ZPC, X2, 128, 256, MINE, (16, 17)),
-        (ZM, X2, 256, 384, MINE, (15, 17)),
-        (ZMC, X2, 256, 384, MINE, (15, 17)),
+        (XP, X0, 64, 384, MINE, (5,)),
+        (ZM, Y2, 0, 128, MINE, (6, 7)),
+        (XP, Y2, 128, 256, MINE, (7, 8)),
+        (ZP, Y2, 256, 384, MINE, (8,)),
+        (ZM, X1, 0, 128, MINE, (9, 10)),
+        (XP, X1, 128, 256, MINE, (10, 13)),
+        (ZP, X1, 256, 384, MINE, (13,)),
+        (ZM, X3, 0, 128, MINE, (11, 12)),
+        (XP, X3, 128, 256, MINE, (12, 14)),
+        (ZP, X3, 256, 384, MINE, (14,)),
+        (ZM, X2, 0, 128, MINE, (15, 16)),
+        (ZMC, X2, 0, 128, MINE, (15, 16)),
+        (XP, X2, 128, 256, MINE, (18, 19)),
+        (XPC, X2, 128, 256, MINE, (18, 19)),
+        (ZP, X2, 256, 384, MINE, (17,)),
+        (ZPC, X2, 256, 384, MINE, (17,)),
         (CORE, OWN, 0, 384, BOTH, ()),
-        (CORE, Y1, 0, 384, BOTH, (0, 1, 18, 19, 20)),
-        (CORE, Y3, 0, 384, BOTH, (2, 3, 21, 22)),
-        (CORE, X0, 0, 384, BOTH, (4, 5, 23, 24)),
-        (CORE, Y2, 0, 384, BOTH, (6, 7, 25, 26)),
-        (CORE, X1, 0, 384, BOTH, (8, 9, 12, 27, 28, 29)),
-        (CORE, X3, 0, 384, MINE, (10, 11, 13)),
-        (CORE, X3, 0, 384, OTHER, (30, 31, 32)),
-        (CORE, X2, 0, 384, MINE, (14, 15, 16, 17)),
+        (CORE, Y1, 0, 384, MINE, (0, 1)),
+        (CORE, Y1, 0, 384, OTHER, (20, 23)),
+        (CORE, Y3, 0, 384, BOTH, (2, 3, 24, 21)),
+        (CORE, X0, 0, 384, BOTH, (4, 5, 25, 22)),
+        (CORE, Y2, 0, 384, BOTH, (6, 7, 8, 26, 27, 28)),
+        (CORE, X1, 0, 384, MINE, (9, 10, 13)),
+        (CORE, X1, 0, 384, OTHER, (29, 30, 31)),
+        (CORE, X3, 0, 384, BOTH, (11, 12, 14, 32, 33, 34)),
+        (CORE, X2, 0, 384, MINE, (15, 16, 17, 18, 19)),
     ),
 )
 ORDER = (
-    (0, 0), (0, 1), (1, 5), (0, 26), (1, 39), (1, 1), (1, 2), (0, 2), (1, 0), (1, 3), (1, 4),
-    (0, 11), (0, 12), (1, 24), (0, 4), (0, 3), (0, 7), (0, 8), (1, 20), (1, 21), (0, 13), (1, 6),
-    (0, 5), (1, 12), (1, 7), (1, 19), (1, 22), (1, 23), (0, 6), (1, 13), (0, 28), (0, 27), (1, 18),
-    (0, 10), (0, 16), (0, 15), (1, 8), (1, 10), (0, 9), (0, 14), (1, 29), (0, 29), (0, 19), (0, 17),
-    (1, 25), (1, 16), (1, 9), (1, 11), (0, 18), (1, 32), (1, 41), (1, 42), (1, 15), (1, 17),
-    (0, 21), (0, 22), (1, 40), (0, 20), (0, 25), (0, 30), (0, 23), (0, 24), (1, 14), (1, 27),
-    (1, 26), (1, 30), (0, 31), (1, 45), (1, 28), (1, 31), (0, 32), (1, 37), (1, 36), (1, 47),
-    (1, 34), (0, 33), (1, 38), (1, 35), (1, 33), (1, 43), (READY, 0), (WORK, 1), (1, 44), (1, 46),
-    (WORK, 17), (READY, 1),
+    (0, 3), (0, 25), (0, 4), (0, 1), (1, 41), (0, 2), (0, 0), (1, 3), (1, 5), (1, 1), (1, 2),
+    (0, 6), (0, 16), (0, 17), (0, 15), (0, 7), (0, 12), (0, 11), (0, 5), (1, 4), (0, 8), (1, 24),
+    (1, 23), (1, 14), (1, 8), (0, 9), (1, 25), (0, 10), (0, 27), (0, 28), (1, 12), (0, 14), (1, 10),
+    (0, 26), (0, 18), (0, 13), (1, 11), (1, 9), (0, 20), (0, 19), (1, 7), (1, 13), (1, 0), (1, 34),
+    (0, 21), (1, 6), (0, 24), (1, 28), (1, 33), (1, 22), (1, 17), (1, 16), (1, 32), (1, 19),
+    (0, 29), (1, 15), (0, 22), (0, 23), (1, 21), (1, 29), (1, 20), (1, 18), (1, 27), (0, 31),
+    (0, 30), (1, 31), (1, 47), (1, 42), (1, 26), (1, 45), (1, 30), (1, 40), (1, 49), (1, 36),
+    (0, 32), (1, 38), (1, 50), (1, 39), (1, 35), (1, 44), (1, 37), (1, 43), (1, 46), (READY, 0),
+    (WORK, 2), (1, 48), (WORK, 16), (READY, 1),
 )
 FIRST, *_, LAST = [k for what, k in ORDER if what == READY]
-
-DIRECT = ()
-FAR, NEAR = (4, 5, 6, 7), (3, 2, 1)
-FINISH = (4, 5, 6, 7, 0, 3, 2, 1)
-
 
 class Place:
     def __init__(self):
@@ -166,7 +163,7 @@
 
 def kernel(
     psi, left, right, source_in, coef_index_in, sixj_in, out, gs, source, coef_index, sixj,
-    lv, rv, hv, acc, sa, ra, sb, rb, sd, rd, load_sem, send_sem, recv_sem, rs_send, rs_recv,
+    lv, rv, hv, acc, sa, ra, sb, load_sem, send_sem, recv_sem, rs_send, rs_recv,
 ):
     here = Place()
     group = here.xh * 4 + here.y
@@ -263,31 +260,28 @@
         )
 
     def along_z(m):
-        src, dst = (sd, rd) if m in DIRECT else (sb, rb)
-        slot = DIRECT.index(m) if m in DIRECT else m - 1
         return pltpu.make_async_remote_copy(
-            src_ref=src.at[slot],
-            dst_ref=dst.at[slot],
-            send_sem=rs_send.at[2 if m in DIRECT else 1],
+            src_ref=sb.at[m],
+            dst_ref=out.at[m],
+            send_sem=rs_send.at[1],
             recv_sem=rs_recv.at[8 + m],
             device_id=here.at(z=places[m]),
             device_id_type=MESH,
         )
 
     def share(m):
-        if m in DIRECT:
-            both = jnp.concatenate([partial_sum(m, mine), partial_sum(m, theirs)], axis=0)
-            sd[DIRECT.index(m)] = both.astype(jnp.bfloat16)
-            along_z(m).start()
-        else:
-            sa[m] = partial_sum(m, theirs).astype(jnp.bfloat16)
-            to_partner(m).start()
+        sa[m] = partial_sum(m, theirs).astype(jnp.bfloat16)
+        to_partner(m).start()
 
     def last_tasks(k):
         tasks = []
-        for half, ms in ((1 - near, FAR), (near, NEAR)):
-            rows = pl.ds(pl.multiple_of(half * (SB // 2), SB // 2), SB // 2)
-            zs = pl.ds(half * 4, 4)
+        for z, count, ms in (
+            (4 * (1 - near), 4, (4, 5, 6, 7)),
+            (4 * near, 4, (3, 2, 1, 0)),
+        ):
+            n = SB // 8
+            rows = pl.ds(pl.multiple_of(z * n, 2 * n), count * n)
+            zs = pl.ds(z, count)
             for s in range(2):
                 tasks += [functools.partial(first, k, p, s, rows) for p in range(NP)]
                 tasks.append(functools.partial(second, k, s, rows, zs))
@@ -327,51 +321,37 @@
     for task in todo:
         task()
 
-    total = None
-    for m in FINISH:
-        if m == 0:
-            total = partial_sum(0, mine)
-            gift = partial_sum(0, theirs)
-            for n in DIRECT:
-                along_z(n).wait_recv()
-                total = total + rd[DIRECT.index(n), : 2 * ROWS].astype(jnp.float32)
-                gift = gift + rd[DIRECT.index(n), 2 * ROWS :].astype(jnp.float32)
-            sa[0] = gift.astype(jnp.bfloat16)
-            to_partner(0).start()
-        else:
-            to_partner(m).wait_recv()
-            sb[m - 1] = (partial_sum(m, mine) + ra[m].astype(jnp.float32)).astype(jnp.bfloat16)
-            along_z(m).start()
-    for m in FINISH:
-        if m == 0:
-            to_partner(0).wait_recv()
-            total = total + ra[0].astype(jnp.float32)
-        else:
-            along_z(m).wait_recv()
-            total = total + rb[m - 1].astype(jnp.float32)
-    out[...] = total.astype(jnp.bfloat16)
-
+    for m in (4, 5, 6, 7, 3, 2, 1):
+        to_partner(m).wait_recv()
+        sb[m] = (partial_sum(m, mine) + ra[m].astype(jnp.float32)).astype(jnp.bfloat16)
+        along_z(m).start()
+    to_partner(0).wait_recv()
+    sb[0] = (partial_sum(0, mine) + ra[0].astype(jnp.float32)).astype(jnp.bfloat16)
+    keep = pltpu.make_async_copy(sb.at[0], out.at[0], rs_recv.at[8])
+    keep.start()
+    for m in (4, 5, 6, 7, 3, 2, 1):
+        along_z(m).wait_recv()
+    keep.wait()
+
+    rb = sb.at[pl.ds(0, 7)]
     for k in range(NCH):
         rows = sum((hi - lo) * (2 if sector == BOTH else 1) for _, _, lo, hi, sector, _ in MESSAGES[k])
         assert rows % SB == 0
         ref = gs[k].at[pl.ds(0, rows // SB)]
         pltpu.make_async_copy(ref, ref, send_sem.at[k]).wait()
-    sent = [(sa.at[pl.ds(0, 8 - len(DIRECT))], 0), (sb.at[pl.ds(0, 7 - len(DIRECT))], 1)]
-    if DIRECT:
-        sent.append((sd, 2))
-    for ref, i in sent:
-        pltpu.make_async_copy(ref, ref, rs_send.at[i]).wait()
+    pltpu.make_async_copy(sa, sa, rs_send.at[0]).wait()
+    pltpu.make_async_copy(rb, rb, rs_send.at[1]).wait()
 
 
 def on_device(psi, left_ops, right_ops, source, coef_index, sixj):
     hbm = pl.BlockSpec(memory_space=pltpu.HBM)
     bf16, f32 = jnp.bfloat16, jnp.float32
-    mine = pl.pallas_call(
+    parts = pl.pallas_call(
         kernel,
         name="sigma",
-        out_shape=jax.ShapeDtypeStruct((2 * ROWS, SB), bf16),
+        out_shape=jax.ShapeDtypeStruct((8, 2 * ROWS, SB), bf16),
         in_specs=[hbm] * 6,
-        out_specs=pl.BlockSpec(memory_space=pltpu.VMEM),
+        out_specs=pl.BlockSpec(memory_space=pl.ANY),
         scratch_shapes=[
             [pltpu.VMEM((32, SB, 128 * w), bf16) for w in WIDTHS],
             pltpu.SMEM((2, NP), jnp.int32),
@@ -383,20 +363,18 @@
             pltpu.VMEM((2, 8, 2, ROWS, SB), f32),
             pltpu.VMEM((8, 2 * ROWS, SB), bf16),
             pltpu.VMEM((8, 2 * ROWS, SB), bf16),
-            pltpu.VMEM((7, 2 * ROWS, SB), bf16),
-            pltpu.VMEM((7, 2 * ROWS, SB), bf16),
-            pltpu.VMEM((max(1, len(DIRECT)), 4 * ROWS, SB), bf16),
-            pltpu.VMEM((max(1, len(DIRECT)), 4 * ROWS, SB), bf16),
+            pltpu.VMEM((8, 2 * ROWS, SB), bf16),
             pltpu.SemaphoreType.DMA((NCH + 5,)),
             pltpu.SemaphoreType.DMA((NCH,)),
             pltpu.SemaphoreType.DMA((NCH, max(len(table) for table in MESSAGES))),
-            pltpu.SemaphoreType.DMA((3,)),
+            pltpu.SemaphoreType.DMA((2,)),
             pltpu.SemaphoreType.DMA((16,)),
         ],
         compiler_params=pltpu.CompilerParams(
             collective_id=0, has_side_effects=True, vmem_limit_bytes=56 * 2**20
         ),
     )(psi, left_ops, right_ops, source.T, coef_index.T, sixj)
+    mine = jnp.sum(parts.astype(f32), axis=0).astype(bf16)
     return jnp.transpose(mine.reshape(2, ROWS, SB), (1, 0, 2))
 
 

time: 49.6 us -> 47.7 us (0.962)
  Pallas kernels: 48 us -> 45.9 us
  other arithmetic: 0 us -> 1.01 us
  local copies, waits for them, and re-layouts: 1.41 us -> 0.65 us
    pallas_call x1, Pallas kernels: 48 us -> 45.9 us  [on_device(): pl.pallas_call(kernel, name='sigma', out_shape=jax.ShapeDtypeStruct((8, 2...]
    reshape x1 -> x0, local copies, waits for them, and re-layouts: 1.41 us -> none  [on_device(): return jnp.transpose(mine.reshape(2, ROWS, SB), (1, 0, 2))]
    reduce_sum x0 -> x1, other arithmetic: none -> 1.01 us  [on_device(): mine = jnp.sum(parts.astype(f32), axis=0).astype(bf16)]
    transpose x0 -> x1, local copies, waits for them, and re-layouts: none -> 0.65 us  [on_device(): return jnp.transpose(mine.reshape(2, ROWS, SB), (1, 0, 2))]
where the time goes in v3:
time: 47.7 us; the launch traced here: 47.6 us
  Pallas kernels  45.9 us (96%)
  other arithmetic  1.01 us (2%)
  local copies, waits for them, and re-layouts  0.65 us (1%)
    pallas_call x1, Pallas kernels, on_device(): pl.pallas_call(kernel, name='sigma', out_shape=jax.ShapeDtypeStruct((8, 2...  45.9 us
    reduce_sum x1, other arithmetic, on_device(): mine = jnp.sum(parts.astype(f32), axis=0).astype(bf16)  1.01 us

profile of v3, /device:TPU:1, one launch (start us, length us, event | category | flops | bytes accessed | tf_op | source)
XLA Modules:
  0.0 47.6 jit_solution(8995849367427610957)
XLA Ops:
  0.0 45.9 %sigma.1 = bf16[8,48,384]{2,1,0:T(8,128)(2,1)} custom-call(bf16[2,384,384]{2,1,0:T(8,128)(2,1)} %psi.1, bf16[8,2,384,384]{3,2,1,0:T(8,128)(2,1)} %left.1, bf16[8,2,384,384]{3,2,1,0:T(8,128)(2,1)} %right.1, s32[2,8]{1,0:T(2,128)} %bitcast.6, s32[2,8]{1,0:T(2,128)} %bitcast.7, f32[64]{0:T(128)} %sixj_in.1), custom_call_target="tpu_custom_call" | custom-call | tf_op jit(solution)/shard_map/sigma/pallas_call | solution.py:349
  45.9 1.0 %reduce_sum.12 = bf16[48,384]{1,0:T(8,128)(2,1)S(1)} reduce(bf16[8,48,384]{2,1,0:T(8,128)(2,1)} %sigma.1, bf16[]{:T(256)} %constant.2.clone.1), dimensions={0}, to_apply=%region_0.0 | reduce | flops 129024 | bytes 331778 | tf_op jit(solution)/shard_map/reduce_sum | solution.py:377
  46.9 0.6 %copy.7 = bf16[24,2,384]{2,1,0:T(2,128)(2,1)} copy(bf16[24,2,384]{2,0,1:T(8,128)(2,1)S(1)} %bitcast.5) | data formatting | bytes 73728 | tf_op jit(solution)/shard_map/transpose | solution.py:378

commit v4 on v3

--- a/solution.py
+++ b/solution.py
@@ -9,7 +9,7 @@
 
 MESH = pl.DeviceIdType.MESH
 SB = 384
-WIDTHS = (1, 2)
+WIDTHS = (2, 1)
 NCH = len(WIDTHS)
 COLS = [slice(128 * sum(WIDTHS[:k]), 128 * sum(WIDTHS[: k + 1])) for k in range(NCH)]
 NP = 8
@@ -22,104 +22,106 @@
 MINE, OTHER, BOTH = range(3)
 MESSAGES = (
     (
-        (YM, OWN, 0, 128, MINE, ()),
-        (YM, OWN, 128, 384, MINE, ()),
-        (YP, OWN, 0, 128, MINE, ()),
-        (YP, OWN, 128, 384, MINE, ()),
-        (XC, OWN, 0, 384, MINE, ()),
-        (YP, Y3, 0, 192, MINE, (2, 3)),
-        (YM, Y1, 192, 384, MINE, (1,)),
+        (YM, OWN, 0, 192, MINE, ()),
+        (YM, OWN, 192, 384, MINE, ()),
+        (YP, OWN, 0, 192, MINE, ()),
+        (YP, OWN, 192, 384, MINE, ()),
+        (XC, OWN, 0, 256, MINE, ()),
+        (XC, OWN, 256, 384, MINE, ()),
+        (YP, Y3, 0, 128, MINE, (2,)),
+        (YP, Y3, 128, 192, MINE, (2,)),
+        (YM, Y1, 192, 256, MINE, (1,)),
+        (YM, Y1, 256, 384, MINE, (1,)),
         (YM, X0, 0, 192, MINE, (4,)),
-        (YM, X0, 192, 320, MINE, (4,)),
         (YP, X0, 0, 192, MINE, (4,)),
-        (YP, X0, 192, 320, MINE, (4,)),
-        (XC, Y1, 320, 384, MINE, (1,)),
-        (XC, Y3, 320, 384, MINE, (3,)),
-        (XC, Y2, 0, 192, MINE, (5,)),
-        (XC, Y2, 192, 384, MINE, (6,)),
-        (ZM, Y1, 0, 384, MINE, (0, 1)),
-        (ZP, Y3, 0, 384, MINE, (2, 3)),
-        (XP, X0, 0, 384, MINE, (4,)),
-        (ZP, Y2, 0, 384, MINE, (5, 6)),
-        (XP, X1, 0, 384, MINE, (7, 8, 11)),
-        (ZM, X3, 0, 192, MINE, (9,)),
-        (ZM, X3, 192, 384, MINE, (10, 12)),
-        (ZP, X2, 0, 128, MINE, (13,)),
-        (XP, X2, 128, 256, MINE, (13, 14)),
-        (ZM, X2, 256, 384, MINE, (14,)),
+        (XC, Y1, 192, 384, MINE, (1,)),
+        (XC, Y3, 192, 384, MINE, (3,)),
+        (YM, X1, 0, 128, MINE, (10,)),
+        (YP, X3, 256, 384, MINE, (13,)),
+        (XC, Y2, 128, 192, MINE, (7,)),
+        (XC, Y2, 192, 256, MINE, (8,)),
+        (YM, OWN, 0, 192, OTHER, ()),
+        (YP, OWN, 0, 192, OTHER, ()),
+        (XP, Y1, 192, 384, MINE, (1,)),
+        (ZP, Y3, 192, 384, MINE, (3,)),
+        (ZM, X0, 0, 128, MINE, (4,)),
+        (XP, X0, 128, 256, MINE, (4,)),
+        (ZP, X0, 256, 384, MINE, (5,)),
+        (ZM, Y2, 0, 128, MINE, (6,)),
+        (XP, Y2, 128, 256, MINE, (7, 8)),
+        (ZP, Y2, 256, 384, MINE, (9,)),
+        (ZM, X1, 0, 128, MINE, (10,)),
+        (XP, X1, 128, 256, MINE, (10, 12)),
+        (ZP, X1, 256, 384, MINE, (12,)),
+        (ZM, X3, 0, 256, MINE, (11, 13)),
+        (ZM, X3, 256, 384, MINE, (13,)),
+        (ZM, X2, 0, 128, MINE, (14,)),
+        (ZMC, X2, 0, 128, MINE, (14,)),
+        (XP, X2, 128, 256, MINE, (16, 17)),
+        (XPC, X2, 128, 256, MINE, (16, 17)),
+        (ZP, X2, 256, 384, MINE, (15,)),
+        (ZPC, X2, 256, 384, MINE, (15,)),
         (CORE, OWN, 0, 384, BOTH, ()),
-        (CORE, Y1, 0, 384, BOTH, (0, 1, 15)),
-        (CORE, Y3, 0, 384, BOTH, (2, 3, 16)),
-        (CORE, X0, 0, 384, BOTH, (4, 17)),
-        (CORE, Y2, 0, 384, BOTH, (5, 6, 18)),
-        (CORE, X1, 0, 384, BOTH, (7, 8, 11, 19)),
-        (CORE, X3, 0, 384, BOTH, (9, 10, 12, 20, 21)),
-        (CORE, X2, 0, 384, BOTH, (13, 14, 22, 23, 24)),
+        (CORE, Y1, 0, 384, MINE, (0, 1)),
+        (CORE, Y1, 0, 384, OTHER, (18, 20)),
+        (CORE, Y3, 0, 384, MINE, (2, 3)),
+        (CORE, Y3, 0, 384, OTHER, (19, 21)),
+        (CORE, X0, 0, 384, BOTH, (4, 5, 22, 23, 24)),
+        (CORE, Y2, 0, 384, MINE, (6, 7, 8, 9)),
+        (CORE, Y2, 0, 384, OTHER, (25, 26, 27)),
+        (CORE, X1, 0, 384, MINE, (10, 12)),
+        (CORE, X1, 0, 384, OTHER, (28, 29, 30)),
+        (CORE, X3, 0, 384, BOTH, (11, 13, 31, 32)),
+        (CORE, X2, 0, 384, MINE, (14, 15, 16, 17)),
     ),
     (
         (YM, OWN, 0, 192, MINE, ()),
         (YM, OWN, 192, 384, MINE, ()),
         (YP, OWN, 0, 192, MINE, ()),
         (YP, OWN, 192, 384, MINE, ()),
-        (XC, OWN, 0, 64, MINE, ()),
-        (XC, OWN, 64, 384, MINE, ()),
-        (YP, Y3, 0, 64, MINE, (2,)),
-        (YP, Y3, 64, 192, MINE, (2,)),
+        (XC, OWN, 0, 320, MINE, ()),
+        (XC, OWN, 320, 384, MINE, ()),
+        (YP, Y3, 0, 192, MINE, (2,)),
         (YM, Y1, 192, 384, MINE, (1,)),
-        (YM, X0, 0, 64, MINE, (4,)),
-        (YM, X0, 64, 192, MINE, (5,)),
-        (YP, X0, 0, 64, MINE, (4,)),
-        (YP, X0, 64, 192, MINE, (5,)),
-        (XC, Y1, 192, 384, MINE, (1,)),
-        (XC, Y3, 192, 384, MINE, (3,)),
-        (YM, X1, 0, 64, MINE, (9,)),
-        (YM, X1, 64, 128, MINE, (10,)),
-        (YP, X3, 256, 384, MINE, (14,)),
-        (XC, Y2, 128, 192, MINE, (7,)),
-        (XC, Y2, 192, 256, MINE, (8,)),
-        (YM, OWN, 0, 192, OTHER, ()),
-        (YP, OWN, 0, 192, OTHER, ()),
-        (XC, OWN, 0, 64, OTHER, ()),
-        (ZP, Y1, 192, 384, MINE, (1,)),
-        (ZM, Y3, 192, 384, MINE, (3,)),
-        (XP, X0, 64, 384, MINE, (5,)),
-        (ZM, Y2, 0, 128, MINE, (6, 7)),
-        (XP, Y2, 128, 256, MINE, (7, 8)),
-        (ZP, Y2, 256, 384, MINE, (8,)),
-        (ZM, X1, 0, 128, MINE, (9, 10)),
-        (XP, X1, 128, 256, MINE, (10, 13)),
-        (ZP, X1, 256, 384, MINE, (13,)),
-        (ZM, X3, 0, 128, MINE, (11, 12)),
-        (XP, X3, 128, 256, MINE, (12, 14)),
-        (ZP, X3, 256, 384, MINE, (14,)),
-        (ZM, X2, 0, 128, MINE, (15, 16)),
-        (ZMC, X2, 0, 128, MINE, (15, 16)),
-        (XP, X2, 128, 256, MINE, (18, 19)),
-        (XPC, X2, 128, 256, MINE, (18, 19)),
-        (ZP, X2, 256, 384, MINE, (17,)),
-        (ZPC, X2, 256, 384, MINE, (17,)),
+        (YM, X0, 0, 320, MINE, (4,)),
+        (YP, X0, 0, 320, MINE, (4,)),
+        (XC, Y1, 320, 384, MINE, (1,)),
+        (XC, Y3, 320, 384, MINE, (3,)),
+        (XC, Y2, 0, 64, MINE, (6,)),
+        (XC, Y2, 64, 192, MINE, (6,)),
+        (XC, Y2, 192, 384, MINE, (7,)),
+        (YM, OWN, 0, 64, OTHER, ()),
+        (YP, OWN, 0, 64, OTHER, ()),
+        (ZM, Y1, 64, 384, MINE, (0, 1)),
+        (ZP, Y3, 64, 384, MINE, (2, 3)),
+        (ZM, X0, 0, 320, MINE, (4,)),
+        (ZM, X0, 320, 384, MINE, (5,)),
+        (XP, Y2, 0, 384, MINE, (6, 7)),
+        (ZP, X1, 0, 384, MINE, (8, 10)),
+        (XP, X3, 0, 384, MINE, (9, 11)),
+        (XP, X2, 0, 128, MINE, (12, 13)),
+        (ZP, X2, 128, 256, MINE, (13, 14)),
+        (ZM, X2, 256, 384, MINE, (14,)),
         (CORE, OWN, 0, 384, BOTH, ()),
-        (CORE, Y1, 0, 384, MINE, (0, 1)),
-        (CORE, Y1, 0, 384, OTHER, (20, 23)),
-        (CORE, Y3, 0, 384, BOTH, (2, 3, 24, 21)),
-        (CORE, X0, 0, 384, BOTH, (4, 5, 25, 22)),
-        (CORE, Y2, 0, 384, BOTH, (6, 7, 8, 26, 27, 28)),
-        (CORE, X1, 0, 384, MINE, (9, 10, 13)),
-        (CORE, X1, 0, 384, OTHER, (29, 30, 31)),
-        (CORE, X3, 0, 384, BOTH, (11, 12, 14, 32, 33, 34)),
-        (CORE, X2, 0, 384, MINE, (15, 16, 17, 18, 19)),
+        (CORE, Y1, 0, 384, BOTH, (0, 1, 17, 15)),
+        (CORE, Y3, 0, 384, BOTH, (2, 3, 18, 16)),
+        (CORE, X0, 0, 384, BOTH, (4, 5, 19, 20)),
+        (CORE, Y2, 0, 384, BOTH, (6, 7, 21)),
+        (CORE, X1, 0, 384, BOTH, (8, 10, 22)),
+        (CORE, X3, 0, 384, BOTH, (9, 11, 23)),
+        (CORE, X2, 0, 384, BOTH, (12, 13, 14, 24, 25, 26)),
     ),
 )
 ORDER = (
-    (0, 3), (0, 25), (0, 4), (0, 1), (1, 41), (0, 2), (0, 0), (1, 3), (1, 5), (1, 1), (1, 2),
-    (0, 6), (0, 16), (0, 17), (0, 15), (0, 7), (0, 12), (0, 11), (0, 5), (1, 4), (0, 8), (1, 24),
-    (1, 23), (1, 14), (1, 8), (0, 9), (1, 25), (0, 10), (0, 27), (0, 28), (1, 12), (0, 14), (1, 10),
-    (0, 26), (0, 18), (0, 13), (1, 11), (1, 9), (0, 20), (0, 19), (1, 7), (1, 13), (1, 0), (1, 34),
-    (0, 21), (1, 6), (0, 24), (1, 28), (1, 33), (1, 22), (1, 17), (1, 16), (1, 32), (1, 19),
-    (0, 29), (1, 15), (0, 22), (0, 23), (1, 21), (1, 29), (1, 20), (1, 18), (1, 27), (0, 31),
-    (0, 30), (1, 31), (1, 47), (1, 42), (1, 26), (1, 45), (1, 30), (1, 40), (1, 49), (1, 36),
-    (0, 32), (1, 38), (1, 50), (1, 39), (1, 35), (1, 44), (1, 37), (1, 43), (1, 46), (READY, 0),
-    (WORK, 2), (1, 48), (WORK, 16), (READY, 1),
+    (0, 4), (1, 1), (1, 2), (1, 27), (0, 39), (1, 0), (1, 3), (1, 15), (0, 3), (0, 1), (1, 4),
+    (1, 6), (0, 5), (1, 7), (1, 17), (1, 18), (0, 2), (0, 23), (0, 10), (1, 5), (0, 22), (1, 11),
+    (1, 10), (0, 13), (0, 21), (1, 9), (1, 19), (0, 20), (1, 8), (0, 24), (1, 21), (1, 14), (0, 11),
+    (1, 28), (1, 20), (0, 8), (1, 13), (0, 9), (0, 42), (0, 28), (1, 12), (0, 7), (0, 12), (0, 0),
+    (0, 6), (0, 32), (1, 23), (1, 22), (1, 30), (0, 44), (1, 26), (1, 16), (0, 17), (0, 14),
+    (0, 15), (1, 25), (1, 31), (0, 31), (1, 24), (0, 27), (0, 26), (0, 16), (0, 18), (0, 19),
+    (0, 45), (0, 25), (0, 29), (0, 30), (1, 33), (0, 47), (1, 29), (0, 40), (1, 32), (1, 34),
+    (0, 35), (0, 33), (0, 37), (0, 50), (0, 36), (0, 38), (0, 34), (0, 49), (0, 41), (0, 43),
+    (0, 48), (READY, 1), (WORK, 1), (0, 46), (WORK, 17), (READY, 0),
 )
 FIRST, *_, LAST = [k for what, k in ORDER if what == READY]
 
@@ -183,13 +185,13 @@
     ]
     load_left = pltpu.make_async_copy(left, lv, load_sem.at[NCH])
     load_right = pltpu.make_async_copy(right, rv, load_sem.at[NCH + 1])
-    for load in loads:
-        load.start()
 
     barrier = pltpu.get_barrier_semaphore()
     adjacent = [here.neighbour(n) for n in LINKS]
     for device in adjacent:
         pl.semaphore_signal(barrier, inc=1, device_id=device, device_id_type=MESH)
+    for load in loads:
+        load.start()
     pl.semaphore_wait(barrier, len(adjacent))
 
     def message(k, i):

time: 47.7 us -> 47.6 us (level)
  no operation moved by 1% of the time
where the time goes in v4:
time: 47.6 us; the launch traced here: 47.4 us
  Pallas kernels  45.8 us (96%)
  other arithmetic  1.01 us (2%)
  local copies, waits for them, and re-layouts  0.65 us (1%)
    pallas_call x1, Pallas kernels, on_device(): pl.pallas_call(kernel, name='sigma', out_shape=jax.ShapeDtypeStruct((8, 2...  45.8 us
    reduce_sum x1, other arithmetic, on_device(): mine = jnp.sum(parts.astype(f32), axis=0).astype(bf16)  1.01 us

profile of v4, /device:TPU:1, one launch (start us, length us, event | category | flops | bytes accessed | tf_op | source)
XLA Modules:
  0.0 47.4 jit_solution(14609456602020975303)
XLA Ops:
  0.0 45.8 %sigma.1 = bf16[8,48,384]{2,1,0:T(8,128)(2,1)} custom-call(bf16[2,384,384]{2,1,0:T(8,128)(2,1)} %psi.1, bf16[8,2,384,384]{3,2,1,0:T(8,128)(2,1)} %left.1, bf16[8,2,384,384]{3,2,1,0:T(8,128)(2,1)} %right.1, s32[2,8]{1,0:T(2,128)} %bitcast.6, s32[2,8]{1,0:T(2,128)} %bitcast.7, f32[64]{0:T(128)} %sixj_in.1), custom_call_target="tpu_custom_call" | custom-call | tf_op jit(solution)/shard_map/sigma/pallas_call | solution.py:351
  45.8 1.0 %reduce_sum.12 = bf16[48,384]{1,0:T(8,128)(2,1)S(1)} reduce(bf16[8,48,384]{2,1,0:T(8,128)(2,1)} %sigma.1, bf16[]{:T(256)} %constant.2.clone.1), dimensions={0}, to_apply=%region_0.0 | reduce | flops 129024 | bytes 331778 | tf_op jit(solution)/shard_map/reduce_sum | solution.py:379
  46.8 0.6 %copy.7 = bf16[24,2,384]{2,1,0:T(2,128)(2,1)} copy(bf16[24,2,384]{2,0,1:T(8,128)(2,1)S(1)} %bitcast.5) | data formatting | bytes 73728 | tf_op jit(solution)/shard_map/transpose | solution.py:380

commit v5 on v4

--- a/solution.py
+++ b/solution.py
@@ -113,7 +113,7 @@
     ),
 )
 ORDER = (
-    (0, 4), (1, 1), (1, 2), (1, 27), (0, 39), (1, 0), (1, 3), (1, 15), (0, 3), (0, 1), (1, 4),
+    (1, 1), (1, 2), (0, 4), (1, 27), (0, 39), (1, 0), (1, 3), (1, 15), (0, 3), (0, 1), (1, 4),
     (1, 6), (0, 5), (1, 7), (1, 17), (1, 18), (0, 2), (0, 23), (0, 10), (1, 5), (0, 22), (1, 11),
     (1, 10), (0, 13), (0, 21), (1, 9), (1, 19), (0, 20), (1, 8), (0, 24), (1, 21), (1, 14), (0, 11),
     (1, 28), (1, 20), (0, 8), (1, 13), (0, 9), (0, 42), (0, 28), (1, 12), (0, 7), (0, 12), (0, 0),
@@ -190,8 +190,8 @@
     adjacent = [here.neighbour(n) for n in LINKS]
     for device in adjacent:
         pl.semaphore_signal(barrier, inc=1, device_id=device, device_id_type=MESH)
-    for load in loads:
-        load.start()
+    for k in dict.fromkeys(k for k, _ in ORDER if k >= 0):
+        loads[k].start()
     pl.semaphore_wait(barrier, len(adjacent))
 
     def message(k, i):

time: 47.6 us -> 48 us (level)
  no operation moved by 1% of the time
where the time goes in v5:
time: 48 us; the launch traced here: 47.9 us
  Pallas kernels  46.2 us (96%)
  other arithmetic  1.01 us (2%)
  local copies, waits for them, and re-layouts  0.65 us (1%)
    pallas_call x1, Pallas kernels, on_device(): pl.pallas_call(kernel, name='sigma', out_shape=jax.ShapeDtypeStruct((8, 2...  46.2 us
    reduce_sum x1, other arithmetic, on_device(): mine = jnp.sum(parts.astype(f32), axis=0).astype(bf16)  1.01 us

profile of v5, /device:TPU:1, one launch (start us, length us, event | category | flops | bytes accessed | tf_op | source)
XLA Modules:
  0.0 47.9 jit_solution(10510388078492877699)
XLA Ops:
  0.0 46.2 %sigma.1 = bf16[8,48,384]{2,1,0:T(8,128)(2,1)} custom-call(bf16[2,384,384]{2,1,0:T(8,128)(2,1)} %psi.1, bf16[8,2,384,384]{3,2,1,0:T(8,128)(2,1)} %left.1, bf16[8,2,384,384]{3,2,1,0:T(8,128)(2,1)} %right.1, s32[2,8]{1,0:T(2,128)} %bitcast.6, s32[2,8]{1,0:T(2,128)} %bitcast.7, f32[64]{0:T(128)} %sixj_in.1), custom_call_target="tpu_custom_call" | custom-call | tf_op jit(solution)/shard_map/sigma/pallas_call | solution.py:351
  46.3 1.0 %reduce_sum.12 = bf16[48,384]{1,0:T(8,128)(2,1)S(1)} reduce(bf16[8,48,384]{2,1,0:T(8,128)(2,1)} %sigma.1, bf16[]{:T(256)} %constant.2.clone.1), dimensions={0}, to_apply=%region_0.0 | reduce | flops 129024 | bytes 331778 | tf_op jit(solution)/shard_map/reduce_sum | solution.py:379
  47.3 0.6 %copy.7 = bf16[24,2,384]{2,1,0:T(2,128)(2,1)} copy(bf16[24,2,384]{2,0,1:T(8,128)(2,1)S(1)} %bitcast.5) | data formatting | bytes 73728 | tf_op jit(solution)/shard_map/transpose | solution.py:380
